TPU v7x, 32 devices: a whole 2x2x4 slice. The times are simulated.
32 devices in a mesh: groups: 2 (over x), tensor: 16 (over z, y, core).
Axes of the slice: x: 2, y: 2, z: 4, core: 2. Of those that a mesh axis runs over, the one named last changes fastest.
Arguments:
- tokens: bfloat16 [256, 4096], P(('groups', 'tensor')), parts along dimension 0, may hold values from -6 to 6
- gate_weight: bfloat16 [8192, 14336], P('groups', 'tensor'), parts along dimension 0, may hold values from -0.09375 to 0.09375
- up_weight: bfloat16 [8192, 14336], P('groups', 'tensor'), parts along dimension 0, may hold values from -0.09375 to 0.09375
- down_weight: bfloat16 [28672, 4096], P(('groups', 'tensor')), parts along dimension 0, may hold values from -0.046875 to 0.046875
- gate_step: bfloat16 [256, 14336], P('groups', 'tensor'), parts along dimension 0, as said below
- up_step: bfloat16 [256, 14336], P('groups', 'tensor'), parts along dimension 0, as said below
- down_step: bfloat16 [896, 4096], P(('groups', 'tensor')), parts along dimension 0, as said below
Outputs:
- gate_grad: bfloat16 [8192, 14336], P('groups', 'tensor'), parts along dimension 0
- up_grad: bfloat16 [8192, 14336], P('groups', 'tensor'), parts along dimension 0
- down_grad: bfloat16 [28672, 4096], P(('groups', 'tensor')), parts along dimension 0
- gate_step_grad: float32 [256, 14336], P('groups', 'tensor'), parts along dimension 0
- up_step_grad: float32 [256, 14336], P('groups', 'tensor'), parts along dimension 0
- down_step_grad: float32 [896, 4096], P(('groups', 'tensor')), parts along dimension 0
There are 2 independent parts, one for each index of `groups`. A program takes and returns all parts, laid end to end along the dimension named above; each array names one. Nothing has to cross between parts.
Inputs may be any that keep to these rules, and one draw needn't show every extreme that they name: `gate_step`: every step size is a power of two. `up_step`: every step size is a power of two. `down_step`: every step size is a power of two.
All inputs are finite; a program needn't handle non-finite values.
Results may differ from a plain program's by a relative error of at most 0.012.
Values may be sent and summed in bfloat16 or wider, within the bound.
A program may use at most 256 MiB of HBM per device.

v0:
```python
import math

import jax
import jax.numpy as jnp
from jax import lax
from jax.sharding import PartitionSpec as P


def fake_quant(weight, step_size):
    group_count, columns = step_size.shape
    step_wide = step_size.astype(jnp.float32)[:, None, :]
    scaled = weight.astype(jnp.float32).reshape(group_count, -1, columns) / step_wide
    levels = jnp.clip(jnp.floor(scaled + 0.5), -8.0, 7.0)
    inside = (scaled >= -8.0) & (scaled <= 7.0)
    fake_weight = (levels * step_wide).reshape(weight.shape).astype(jnp.bfloat16)
    step_slope = jnp.where(inside, levels - scaled, levels)
    return (fake_weight, inside, step_slope)


def latent_grads(full_grad, inside, step_slope):
    group_count = inside.shape[0]
    columns = inside.shape[2]
    shaped = full_grad.reshape(group_count, -1, columns)
    latent = jnp.where(inside, shaped, 0.0).reshape(full_grad.shape).astype(jnp.bfloat16)
    step_grad = jnp.sum(shaped * step_slope, axis=1) * (1.0 / math.sqrt(shaped.shape[1] * 7.0))
    return (latent, step_grad)


def body(tokens, gate_weight, up_weight, down_weight, gate_step, up_step, down_step):
    whole = lax.all_gather(tokens, "tensor", axis=0, tiled=True)
    gate_fake, gate_inside, gate_slope = fake_quant(gate_weight, gate_step)
    up_fake, up_inside, up_slope = fake_quant(up_weight, up_step)
    down_fake, down_inside, down_slope = fake_quant(down_weight, down_step)
    teacher_gate = jnp.dot(whole, gate_weight, preferred_element_type=jnp.float32)
    teacher_up = jnp.dot(whole, up_weight, preferred_element_type=jnp.float32)
    teacher_hidden = (jax.nn.silu(teacher_gate) * teacher_up).astype(jnp.bfloat16)
    gate_pre = jnp.dot(whole, gate_fake, preferred_element_type=jnp.float32)
    up_pre = jnp.dot(whole, up_fake, preferred_element_type=jnp.float32)
    sigmoid_gate = jax.nn.sigmoid(gate_pre)
    silu_gate = gate_pre * sigmoid_gate
    hidden = (silu_gate * up_pre).astype(jnp.bfloat16)
    hidden_rows = hidden
    difference = lax.psum_scatter(
        jnp.dot(hidden_rows, down_fake, preferred_element_type=jnp.float32)
        - jnp.dot(teacher_hidden, down_weight, preferred_element_type=jnp.float32),
        "tensor",
        scatter_dimension=0,
        tiled=True,
    )
    error = difference.astype(jnp.bfloat16)
    incoming = lax.all_gather(error, "tensor", axis=0, tiled=True)
    hidden_rows = hidden
    down_total = lax.dot_general(
        hidden_rows, incoming, (((0,), (0,)), ((), ())), preferred_element_type=jnp.float32
    )
    rows_grad = lax.dot_general(
        incoming, down_fake, (((1,), (1,)), ((), ())), preferred_element_type=jnp.float32
    )
    hidden_grad = rows_grad
    down_full, hidden_grad = (down_total, hidden_grad)
    gate_pre_grad = (
        hidden_grad * up_pre * sigmoid_gate * (1.0 + gate_pre * (1.0 - sigmoid_gate))
    ).astype(jnp.bfloat16)
    up_pre_grad = (hidden_grad * silu_gate).astype(jnp.bfloat16)
    gate_full = lax.dot_general(
        whole, gate_pre_grad, (((0,), (0,)), ((), ())), preferred_element_type=jnp.float32
    )
    up_full = lax.dot_general(
        whole, up_pre_grad, (((0,), (0,)), ((), ())), preferred_element_type=jnp.float32
    )
    gate_grad, gate_step_grad = latent_grads(gate_full, gate_inside, gate_slope)
    up_grad, up_step_grad = latent_grads(up_full, up_inside, up_slope)
    down_grad, down_step_grad = latent_grads(down_full, down_inside, down_slope)
    return (gate_grad, up_grad, down_grad, gate_step_grad, up_step_grad, down_step_grad)


def solution(mesh):
    return jax.shard_map(
        body,
        mesh=mesh,
        in_specs=(
            P(("groups", "tensor"), None),
            P("groups", "tensor"),
            P("groups", "tensor"),
            P(("groups", "tensor"), None),
            P("groups", "tensor"),
            P("groups", "tensor"),
            P(("groups", "tensor"), None),
        ),
        out_specs=(
            P("groups", "tensor"),
            P("groups", "tensor"),
            P(("groups", "tensor"), None),
            P("groups", "tensor"),
            P("groups", "tensor"),
            P(("groups", "tensor"), None),
        ),
        check_vma=False,
    )
```

profile of v0, /device:TPU:0, one launch (start us, length us, event | category | flops | bytes accessed | tf_op | source)
XLA Modules:
  0.0 359.2 jit_solution(2102738082270516531)
XLA Ops:
  8.0 10.8 %copy.23 = bf16[4096,896]{0,1:T(8,128)(2,1)} copy(bf16[4096,896]{1,0:T(8,128)(2,1)} %param.8) | data formatting | bytes 14680064 | tf_op args[1]
  18.7 6.1 %div.49 = f32[128,32,896]{2,1,0:T(8,128)} broadcast(bf16[128,896]{1,0:T(8,128)(2,1)S(1)} %copy-done.8), dimensions={0,2} | broadcast | bytes 14909440 | tf_op jit(solution)/shard_map/div | solution.py:12
  24.8 16.1 %copy.24 = f32[4096,896]{0,1:T(8,128)} copy(f32[4096,896]{1,0:T(8,128)} %bitcast.50) | data formatting | bytes 29360128 | tf_op jit(solution)/shard_map/div | solution.py:12
  41.0 10.9 %copy.26 = bf16[4096,896]{0,1:T(8,128)(2,1)} copy(bf16[4096,896]{1,0:T(8,128)(2,1)} %param.9) | data formatting | bytes 14680064 | tf_op args[2]
  51.9 6.1 %div.53 = f32[128,32,896]{2,1,0:T(8,128)} broadcast(bf16[128,896]{1,0:T(8,128)(2,1)S(1)} %copy-done.6), dimensions={0,2} | broadcast | bytes 14909440 | tf_op jit(solution)/shard_map/div | solution.py:12
  58.0 16.2 %copy.27 = f32[4096,896]{0,1:T(8,128)} copy(f32[4096,896]{1,0:T(8,128)} %bitcast.51) | data formatting | bytes 29360128 | tf_op jit(solution)/shard_map/div | solution.py:12
  75.0 8.2 %fusion.6 = bf16[896,4096]{1,0:T(8,128)(2,1)} fusion(f32[28,4096]{1,0:T(8,128)S(1)} %convert_element_type.59, bf16[896,4096]{1,0:T(8,128)(2,1)} %param.10), kind=kLoop, calls=%fused_computation.11 | loop fusion | flops 25690112 | bytes 15138816 | tf_op jit(solution)/shard_map/convert_element_type | solution.py:15
  83.2 9.8 %fusion.14 = f32[128,896]{0,1:T(8,128)S(1)} fusion(bf16[128,4096]{1,0:T(8,128)(2,1)} %all-gather.3.cloned.1.call-done, f32[4096,896]{0,1:T(8,128)} %copy.24, bf16[4096,896]{0,1:T(8,128)(2,1)} %copy.23), kind=kOutput, calls=%fused_computation.28 | convolution fusion | flops 965214208 | bytes 23527424 | tf_op jit(solution)/shard_map/dot_general | solution.py:37
  95.1 7.2 %multiply_convert_fusion.10 = (bf16[128,896]{0,1:T(8,128)(2,1)S(1)}, f32[128,896]{0,1:T(8,128)}) fusion(f32[128,896]{0,1:T(8,128)S(1)} %fusion.14, bf16[128,4096]{1,0:T(8,128)(2,1)S(1)} %copy-done.3, f32[4096,896]{0,1:T(8,128)S(1)} %copy-done, bf16[4096,896]{0,1:T(8,128)(2,1)} %copy.26), kind=kOutput, calls=%fused_computation.37 | convolution fusion | flops 965902336 | bytes 24215552 | tf_op jit(solution)/shard_map/dot_general | solution.py:38
  109.3 12.0 %convolution_subtract_fusion = f32[128,4096]{1,0:T(8,128)} fusion(f32[128,4096]{1,0:T(8,128)S(1)} %fusion.34, bf16[896,4096]{1,0:T(8,128)(2,1)} %param.10, bf16[128,4096]{1,0:T(8,128)(2,1)S(1)} %copy-done.3, bf16[4096,896]{1,0:T(8,128)(2,1)} %param.9, f32[128,896]{0,1:T(8,128)} %fusion.35), kind=kOutput, calls=%fused_computation.25 | convolution fusion | flops 1880260608 | bytes 20381696 | tf_op jit(solution)/shard_map/dot_general | solution.py:45
  121.4 64.3 %reduce-scatter.2.cloned.1.call-done = f32[8,4096]{1,0:T(8,128)} async-done(((f32[128,4096]{1,0:T(8,128)}), f32[8,4096]{1,0:T(8,128)}) %reduce-scatter.2.cloned.1.call-update) | async-done | bytes 131088 | tf_op jit(solution)/shard_map/reduce_scatter | solution.py:43
  187.3 11.9 %copy.36 = f32[4096,896]{1,0:T(8,128)} copy(bf16[4096,896]{0,1:T(8,128)(2,1)} %copy.26) | data formatting | bytes 22020096 | tf_op jit(solution)/shard_map/convert_element_type | solution.py:12
  200.0 11.7 %copy.34 = f32[4096,896]{1,0:T(8,128)} copy(bf16[4096,896]{0,1:T(8,128)(2,1)} %copy.23) | data formatting | bytes 22020096 | tf_op jit(solution)/shard_map/convert_element_type | solution.py:12
  212.5 12.6 %all-gather.5.cloned.1.call-done = bf16[128,4096]{1,0:T(8,128)(2,1)} async-done(((bf16[8,4096]{1,0:T(8,128)(2,1)}), bf16[128,4096]{1,0:T(8,128)(2,1)}) %all-gather.5.cloned.1.call-update) | async-done | bytes 1048592 | tf_op jit(solution)/shard_map/all_gather | solution.py:51
  230.6 13.8 %select_convert_fusion.1 = (bf16[4096,896]{0,1:T(8,128)(2,1)}, f32[4096,896]{0,1:T(8,128)}) fusion(f32[4096,896]{0,1:T(8,128)} %copy.27, bf16[4096,896]{0,1:T(8,128)(2,1)} %copy.26, bf16[128,4096]{1,0:T(8,128)(2,1)S(1)} %copy-done.3, f32[128,896]{0,1:T(8,128)S(1)} %fusion.36, f32[128,896]{0,1:T(8,128)S(1)} %copy-done.12), kind=kOutput, calls=%fused_computation.13 | convolution fusion | flops 962232320 | bytes 46006272 | tf_op jit(solution)/shard_map/dot_general | solution.py:68
  244.3 16.2 %copy.35 = f32[4096,896]{1,0:T(8,128)} copy(f32[4096,896]{0,1:T(8,128)} %get-tuple-element.23) | data formatting | bytes 29360128 | tf_op jit(solution)/shard_map/dot_general | solution.py:68
  260.5 13.9 %select_convert_fusion.2 = (bf16[4096,896]{0,1:T(8,128)(2,1)}, f32[4096,896]{0,1:T(8,128)}) fusion(f32[4096,896]{0,1:T(8,128)} %copy.24, bf16[4096,896]{0,1:T(8,128)(2,1)} %copy.23, bf16[128,4096]{1,0:T(8,128)(2,1)S(1)} %copy-done.3, f32[128,896]{0,1:T(8,128)S(1)} %copy-done.12, f32[128,896]{0,1:T(8,128)S(1)} %fusion.36, f32[128,896]{0,1:T(8,128)S(1)} %copy-done.13), kind=kOutput, calls=%fused_computation.14 | convolution fusion | flops 962691072 | bytes 46465024 | tf_op jit(solution)/shard_map/dot_general | solution.py:65
  274.4 16.3 %copy.33 = f32[4096,896]{1,0:T(8,128)} copy(f32[4096,896]{0,1:T(8,128)} %get-tuple-element.21) | data formatting | bytes 29360128 | tf_op jit(solution)/shard_map/dot_general | solution.py:65
  290.7 8.1 %select_convert_fusion = (bf16[896,4096]{1,0:T(8,128)(2,1)}, f32[896,4096]{1,0:T(8,128)S(1)}) fusion(f32[28,4096]{1,0:T(8,128)} %copy-done.1, bf16[896,4096]{1,0:T(8,128)(2,1)} %param.10, bf16[128,896]{0,1:T(8,128)(2,1)S(1)} %get-tuple-element.18, bf16[128,4096]{1,0:T(8,128)(2,1)} %all-gather.5.cloned.1.call-done), kind=kOutput, calls=%fused_computation.12 | convolution fusion | flops 961544192 | bytes 31096832 | tf_op jit(solution)/shard_map/dot_general | solution.py:53
  298.8 6.9 %fusion.5 = f32[28,4096]{1,0:T(8,128)S(1)} fusion(f32[28,32,4096]{2,1,0:T(8,128)S(1)} %bitcast.52, f32[28,4096]{1,0:T(8,128)S(1)} %copy-done.2, bf16[28,32,4096]{2,1,0:T(8,128)(2,1)S(1)} %bitcast.49), kind=kLoop, calls=%fused_computation.10 | loop fusion | flops 43925504 | bytes 22937600 | tf_op jit(solution)/shard_map/reduce_sum | solution.py:25
  306.6 10.9 %copy.37 = bf16[4096,896]{1,0:T(8,128)(2,1)} copy(bf16[4096,896]{0,1:T(8,128)(2,1)} %get-tuple-element.20) | data formatting | bytes 14680064
  317.4 10.8 %copy.38 = bf16[4096,896]{1,0:T(8,128)(2,1)} copy(bf16[4096,896]{0,1:T(8,128)(2,1)} %get-tuple-element.22) | data formatting | bytes 14680064
  328.3 11.7 %fusion.3 = f32[128,896]{1,0:T(8,128)S(1)} fusion(f32[128,896]{1,0:T(8,128)S(1)} %copy-done.5, f32[4096,896]{1,0:T(8,128)} %copy.36, f32[4096,896]{1,0:T(8,128)} %copy.35), kind=kLoop, calls=%fused_computation.8 | loop fusion | flops 40255488 | bytes 30277632 | tf_op jit(solution)/shard_map/reduce_sum | solution.py:25
  340.0 11.7 %fusion.1 = f32[128,896]{1,0:T(8,128)S(1)} fusion(f32[128,896]{1,0:T(8,128)S(1)} %copy-done.4, f32[4096,896]{1,0:T(8,128)} %copy.34, f32[4096,896]{1,0:T(8,128)} %copy.33), kind=kLoop, calls=%fused_computation.6 | loop fusion | flops 40255488 | bytes 30277632 | tf_op jit(solution)/shard_map/reduce_sum | solution.py:25
  (59 shorter events, 21.2 us)
Async XLA Ops:
  7.2 11.6 %copy-start.8 = (bf16[128,896]{1,0:T(8,128)(2,1)S(1)}, bf16[128,896]{1,0:T(8,128)(2,1)}, u32[]{:S(2)}) copy-start(bf16[128,896]{1,0:T(8,128)(2,1)} %param.11) | copy-start | bytes 688132
  7.2 76.0 %all-gather.3.cloned.1.call-start = ((), (), s32[]{:S(2)}) async-start(), calls=%async_computation.1 | async-start | bytes 1114112 | tf_op jit(solution)/shard_map/all_gather | solution.py:30
  7.9 177.8 %reduce-scatter.2.cloned.1.call-start = ((), (), s32[]{:S(2)}) async-start(), calls=%async_computation.2 | async-start | bytes 2228224 | tf_op jit(solution)/shard_map/reduce_scatter | solution.py:43
  41.0 10.9 %copy-start.6 = (bf16[128,896]{1,0:T(8,128)(2,1)S(1)}, bf16[128,896]{1,0:T(8,128)(2,1)}, u32[]{:S(2)}) copy-start(bf16[128,896]{1,0:T(8,128)(2,1)} %param.12) | copy-start | bytes 688132
  58.0 16.2 %copy-start.10 = (bf16[28,4096]{1,0:T(8,128)(2,1)S(1)}, bf16[28,4096]{1,0:T(8,128)(2,1)}, u32[]{:S(2)}) copy-start(bf16[28,4096]{1,0:T(8,128)(2,1)} %param.13) | copy-start | bytes 688132
  74.2 0.8 copy-start.1
  83.2 11.7 %copy-start = (f32[4096,896]{0,1:T(8,128)S(1)}, f32[4096,896]{0,1:T(8,128)}, u32[]{:S(2)}) copy-start(f32[4096,896]{0,1:T(8,128)} %copy.27) | copy-start | bytes 44040196
  83.2 12.0 %copy-start.3 = (bf16[128,4096]{1,0:T(8,128)(2,1)S(1)}, bf16[128,4096]{1,0:T(8,128)(2,1)}, u32[]{:S(2)}) copy-start(bf16[128,4096]{1,0:T(8,128)(2,1)} %all-gather.3.cloned.1.call-done) | copy-start | bytes 3145732
  83.2 19.2 %slice-start = ((s8[7340032]{0:T(1024)(128)(4,1)}), s8[4194304]{0:T(1024)(128)(4,1)S(1)}, s32[]{:S(2)}) async-start(s8[7340032]{0:T(1024)(128)(4,1)} %bitcast.45), calls=%async_computation.4 | async-start | bytes 8388608
  95.1 7.2 %copy-start.11 = (f32[128,896]{0,1:T(8,128)}, f32[128,896]{0,1:T(8,128)S(1)}, u32[]{:S(2)}) copy-start(f32[128,896]{0,1:T(8,128)S(1)} %fusion.14) | copy-start | bytes 1376260
  95.1 7.3 %slice-start.1 = ((s8[7340032]{0:T(1024)(128)(4,1)}), s8[3145728]{0:T(1024)(128)(4,1)S(1)}, s32[]{:S(2)}) async-start(s8[7340032]{0:T(1024)(128)(4,1)} %bitcast.45), calls=%async_computation.5 | async-start | bytes 6291456
  102.4 2.2 slice-start.4
  102.4 3.1 slice-start.5
  121.3 77.9 %copy-start.7 = (bf16[128,896]{1,0:T(8,128)(2,1)S(1)}, bf16[128,896]{1,0:T(8,128)(2,1)}, u32[]{:S(2)}) copy-start(bf16[128,896]{1,0:T(8,128)(2,1)} %param.12) | copy-start | bytes 688132
  121.3 103.7 %all-gather.5.cloned.1.call-start = ((), (), s32[]{:S(2)}) async-start(), calls=%async_computation.3 | async-start | bytes 1114112 | tf_op jit(solution)/shard_map/all_gather | solution.py:51
  199.2 12.5 %copy-start.9 = (bf16[128,896]{1,0:T(8,128)(2,1)S(1)}, bf16[128,896]{1,0:T(8,128)(2,1)}, u32[]{:S(2)}) copy-start(bf16[128,896]{1,0:T(8,128)(2,1)} %param.11) | copy-start | bytes 688132
  200.0 30.6 %copy-start.12 = (f32[128,896]{0,1:T(8,128)S(1)}, f32[128,896]{0,1:T(8,128)}, u32[]{:S(2)}) copy-start(f32[128,896]{0,1:T(8,128)} %copy-done.11) | copy-start | bytes 1376260
  244.3 16.2 %copy-start.13 = (f32[128,896]{0,1:T(8,128)S(1)}, f32[128,896]{0,1:T(8,128)}, u32[]{:S(2)}) copy-start(f32[128,896]{0,1:T(8,128)} %get-tuple-element.19) | copy-start | bytes 1376260
  274.4 24.4 %slice-start.2 = ((s8[7340032]{0:T(1024)(128)(4,1)}), s8[3145728]{0:T(1024)(128)(4,1)S(1)}, s32[]{:S(2)}) async-start(s8[7340032]{0:T(1024)(128)(4,1)} %bitcast.47), calls=%async_computation.6 | async-start | bytes 6291456
  290.7 8.1 %slice-start.3 = ((s8[7340032]{0:T(1024)(128)(4,1)}), s8[4194304]{0:T(1024)(128)(4,1)S(1)}, s32[]{:S(2)}) async-start(s8[7340032]{0:T(1024)(128)(4,1)} %bitcast.47), calls=%async_computation.7 | async-start | bytes 8388608
  290.7 8.1 %copy-start.2 = (f32[28,4096]{1,0:T(8,128)S(1)}, f32[28,4096]{1,0:T(8,128)}, u32[]{:S(2)}) copy-start(f32[28,4096]{1,0:T(8,128)} %copy-done.1) | copy-start | bytes 1376260
  306.6 21.7 %copy-start.5 = (f32[128,896]{1,0:T(8,128)S(1)}, f32[128,896]{1,0:T(8,128)}, u32[]{:S(2)}) copy-start(f32[128,896]{1,0:T(8,128)} %convert_element_type.55) | copy-start | bytes 1376260
  328.3 11.7 %copy-start.4 = (f32[128,896]{1,0:T(8,128)S(1)}, f32[128,896]{1,0:T(8,128)}, u32[]{:S(2)}) copy-start(f32[128,896]{1,0:T(8,128)} %convert_element_type.52) | copy-start | bytes 1376260
Sparse Core Ops, SparseCore 0:
  10.2 40.6 all-gather.2
  121.5 64.2 reduce-scatter.1
  188.1 36.9 all-gather.4
where the time goes:
time: 362 us; the launch traced here: 359 us
  local copies, waits for them, and re-layouts  149 us (41%)
  waiting for transfers between devices  77.6 us (21%)
  matrix products  75.3 us (21%)
  other arithmetic  43.5 us (12%)
  between operations  13.9 us (4%)
    reduce_scatter x1, waiting for transfers between devices, body(): lax.psum_scatter(jnp.dot(hidden_rows, down_fake, preferred_element_type=j...  64.3 us
    unnamed x44, local copies, waits for them, and re-layouts  48.2 us
    div x4, local copies, waits for them, and re-layouts, fake_quant(): weight.astype(jnp.float32).reshape(group_count, -1, columns) / step_wide  44.5 us
    reduce_sum x3, other arithmetic, latent_grads(): jnp.sum(shaped * step_slope, axis=1)  30.3 us
    convert_element_type x2, local copies, waits for them, and re-layouts, fake_quant(): weight.astype(jnp.float32).reshape(group_count, -1, columns) / step_wide  23.6 us
    dot_general x1, local copies, waits for them, and re-layouts, body(): lax.dot_general(whole, gate_pre_grad, (((0,), (0,)), ((), ())), preferred...  16.3 us
    dot_general x1, local copies, waits for them, and re-layouts, body(): lax.dot_general(whole, up_pre_grad, (((0,), (0,)), ((), ())), preferred_e...  16.2 us
    dot_general x1, matrix products, body(): lax.dot_general(whole, gate_pre_grad, (((0,), (0,)), ((), ())), preferred...  13.9 us
  transfers between devices with their start and end apart: 3, of which 2 were waited for; matrix products, arithmetic and copies ran while one was open for 28% of the time, Pallas kernels for 0%

commit v1 on v0

v1 whole, which is shorter than its diff:
```python
import functools
import math

import jax
import jax.numpy as jnp
from jax import lax
from jax.experimental import pallas as pl
from jax.experimental.pallas import tpu as pltpu
from jax.sharding import PartitionSpec as P

F32 = jnp.float32
BF16 = jnp.bfloat16
MESH = pl.DeviceIdType.MESH
GROUP = 32
CHUNKS = 4
VMEM_LIMIT = 56 * 1024 * 1024


def place(Z, Y):
    me = lax.axis_index("tensor")
    core = lax.rem(me, 2)
    y = lax.rem(me // 2, Y)
    z = me // (2 * Y)
    return z, y, core


def meet(Z, Y, z, y, core):
    peers = [(lax.rem(z + d, Z) * Y + y) * 2 + core for d in range(1, Z)]
    peers.append((z * Y + (1 - y)) * 2 + core)
    peers.append((z * Y + y) * 2 + (1 - core))
    barrier = pltpu.get_barrier_semaphore()
    for peer in peers:
        pl.semaphore_signal(barrier, inc=1, device_id={"tensor": peer}, device_id_type=MESH)
    pl.semaphore_wait(barrier, len(peers))
    return peers


def remote(src, dst, send, recv, peer):
    return pltpu.make_async_remote_copy(
        src_ref=src, dst_ref=dst, send_sem=send, recv_sem=recv,
        device_id={"tensor": peer}, device_id_type=MESH,
    )


def spread_line(out, cols, sems, k, base, Z, z, y, core, peers):
    send, recv = sems
    copies = []
    for d in range(Z - 1):
        part = out.at[z, y, core, :, cols]
        copies.append(remote(part, part, send.at[k, base + d], recv.at[k, base + d], peers[d]))
        copies[-1].start()
    return copies


def spread_rest(out, chunks, line, sems, base, Z, z, y, core, peers):
    send, recv = sems
    rows, pair = [], []
    for k, cols in enumerate(chunks):
        for copy in line[k]:
            copy.wait_recv()
        part = out.at[:, y, core, :, cols]
        rows.append(remote(part, part, send.at[k, base], recv.at[k, base], peers[Z - 1]))
        rows[-1].start()
    for k, cols in enumerate(chunks):
        rows[k].wait_recv()
        part = out.at[:, :, core, :, cols]
        pair.append(remote(part, part, send.at[k, base + 1], recv.at[k, base + 1], peers[Z]))
        pair[-1].start()
    for k in range(len(chunks)):
        pair[k].wait_recv()
        for copy in line[k] + [rows[k], pair[k]]:
            copy.wait_send()


def gather_kernel(Z, Y, x_ref, out, send, recv):
    z, y, core = place(Z, Y)
    width = x_ref.shape[1] // CHUNKS
    chunks = [pl.ds(k * width, width) for k in range(CHUNKS)]
    out[z, y, core] = x_ref[...]
    peers = meet(Z, Y, z, y, core)
    line = [
        spread_line(out, cols, (send, recv), k, 0, Z, z, y, core, peers)
        for k, cols in enumerate(chunks)
    ]
    spread_rest(out, chunks, line, (send, recv), Z - 1, Z, z, y, core, peers)


def sum_gather_kernel(Z, Y, p_ref, out, from_core, to_y, mine, from_y, to_z, from_z, send, recv):
    z, y, core = place(Z, Y)
    width = p_ref.shape[-1] // CHUNKS
    chunks = [pl.ds(k * width, width) for k in range(CHUNKS)]
    peers = meet(Z, Y, z, y, core)
    waiting = []
    first = []
    for k, cols in enumerate(chunks):
        copy = remote(
            p_ref.at[:, :, 1 - core, :, cols], from_core.at[:, :, :, cols],
            send.at[k, 0], recv.at[k, 0], peers[Z],
        )
        copy.start()
        first.append(copy)
    second = []
    for k, cols in enumerate(chunks):
        first[k].wait_recv()
        for i in range(Z):
            to_y[i, :, cols] = (
                p_ref[i, 1 - y, core, :, cols].astype(F32)
                + from_core[i, 1 - y, :, cols].astype(F32)
            ).astype(BF16)
        copy = remote(
            to_y.at[:, :, cols], from_y.at[:, :, cols], send.at[k, 1], recv.at[k, 1], peers[Z - 1]
        )
        copy.start()
        second.append(copy)
        for i in range(Z):
            mine[i, :, cols] = (
                p_ref[i, y, core, :, cols].astype(F32) + from_core[i, y, :, cols].astype(F32)
            )
    third = []
    for k, cols in enumerate(chunks):
        second[k].wait_recv()
        for i in range(Z):
            mine[i, :, cols] = mine[i, :, cols] + from_y[i, :, cols].astype(F32)
        third.append([])
        for d in range(Z - 1):
            there = lax.rem(z + d + 1, Z)
            to_z[d, :, cols] = mine[there, :, cols].astype(BF16)
            copy = remote(
                to_z.at[d, :, cols], from_z.at[d, :, cols],
                send.at[k, 2 + d], recv.at[k, 2 + d], peers[d],
            )
            copy.start()
            third[k].append(copy)
    line = []
    for k, cols in enumerate(chunks):
        total = mine[z, :, cols]
        for d in range(Z - 1):
            third[k][d].wait_recv()
            total = total + from_z[d, :, cols].astype(F32)
        out[z, y, core, :, cols] = total.astype(BF16)
        line.append(spread_line(out, cols, (send, recv), k, Z + 1, Z, z, y, core, peers))
    spread_rest(out, chunks, line, (send, recv), 2 * Z, Z, z, y, core, peers)
    for k in range(CHUNKS):
        for copy in [first[k], second[k]] + third[k]:
            copy.wait_send()


def split_axis(count):
    return count // 4, 2


def gather_tokens(tokens, count):
    Z, Y = split_axis(count)
    rows, width = tokens.shape
    out = pl.pallas_call(
        functools.partial(gather_kernel, Z, Y),
        out_shape=jax.ShapeDtypeStruct((Z, Y, 2, rows, width), BF16),
        in_specs=[pl.BlockSpec(memory_space=pltpu.VMEM)],
        out_specs=pl.BlockSpec(memory_space=pltpu.VMEM),
        scratch_shapes=[
            pltpu.SemaphoreType.DMA((CHUNKS, Z + 1)),
            pltpu.SemaphoreType.DMA((CHUNKS, Z + 1)),
        ],
        compiler_params=pltpu.CompilerParams(
            collective_id=0, has_side_effects=True, vmem_limit_bytes=VMEM_LIMIT
        ),
        name="gather_tokens",
    )(tokens)
    return out.reshape(count * rows, width)


def sum_gather(partial, count):
    Z, Y = split_axis(count)
    width = partial.shape[1]
    rows = partial.shape[0] // count
    out = pl.pallas_call(
        functools.partial(sum_gather_kernel, Z, Y),
        out_shape=jax.ShapeDtypeStruct((Z, Y, 2, rows, width), BF16),
        in_specs=[pl.BlockSpec(memory_space=pltpu.VMEM)],
        out_specs=pl.BlockSpec(memory_space=pltpu.VMEM),
        scratch_shapes=[
            pltpu.VMEM((Z, Y, rows, width), BF16),
            pltpu.VMEM((Z, rows, width), BF16),
            pltpu.VMEM((Z, rows, width), F32),
            pltpu.VMEM((Z, rows, width), BF16),
            pltpu.VMEM((Z - 1, rows, width), BF16),
            pltpu.VMEM((Z - 1, rows, width), BF16),
            pltpu.SemaphoreType.DMA((CHUNKS, 2 * Z + 2)),
            pltpu.SemaphoreType.DMA((CHUNKS, 2 * Z + 2)),
        ],
        compiler_params=pltpu.CompilerParams(
            collective_id=1, has_side_effects=True, vmem_limit_bytes=VMEM_LIMIT
        ),
        name="sum_gather_error",
    )(partial.reshape(Z, Y, 2, rows, width))
    return out.reshape(partial.shape)


def prepare_steps(s_ref, s_scr, r_scr):
    steps = s_ref[...].astype(F32)
    s_scr[...] = steps
    r_scr[...] = 1.0 / steps


def quantize(w_ref, s_scr, r_scr, fake):
    for g in range(s_scr.shape[0]):
        rows = pl.ds(g * GROUP, GROUP)
        scaled = w_ref[rows, :].astype(F32) * r_scr[pl.ds(g, 1), :]
        levels = jnp.floor(jnp.clip(scaled, -8.0, 7.0) + 0.5)
        fake[rows, :] = (levels * s_scr[pl.ds(g, 1), :]).astype(BF16)


def latent(w_ref, s_scr, r_scr, full, grad_ref, step_ref, fake=None):
    factor = 1.0 / math.sqrt(GROUP * 7.0)
    for g in range(s_scr.shape[0]):
        rows = pl.ds(g * GROUP, GROUP)
        scaled = w_ref[rows, :].astype(F32) * r_scr[pl.ds(g, 1), :]
        clipped = jnp.clip(scaled, -8.0, 7.0)
        levels = jnp.floor(clipped + 0.5)
        inside = clipped == scaled
        if fake is not None:
            fake[rows, :] = (levels * s_scr[pl.ds(g, 1), :]).astype(BF16)
        part = full[rows, :]
        grad_ref[rows, :] = jnp.where(inside, part, 0.0).astype(BF16)
        slope = levels - jnp.where(inside, scaled, 0.0)
        step_ref[pl.ds(g, 1), :] = jnp.sum(part * slope, axis=0, keepdims=True) * factor


def dot(a, b):
    return jnp.dot(a, b, preferred_element_type=F32)


def forward_kernel(
    T, tok, gw, uw, dw, gs, us, ds,
    partial, gate_pre, up_pre, hidden,
    tg, tu, th, s_scr, r_scr, sd_scr, rd_scr, fake, fake_d,
):
    i = pl.program_id(0)

    @pl.when(i == 0)
    def _():
        for ref in (tg, tu, gate_pre, up_pre):
            ref[...] = jnp.zeros_like(ref)

    @pl.when(i < T)
    def _():
        x = tok[...]
        for w, s, teacher, pre in ((gw, gs, tg, gate_pre), (uw, us, tu, up_pre)):
            prepare_steps(s, s_scr, r_scr)
            quantize(w, s_scr, r_scr, fake)
            teacher[...] += dot(x, w[...])
            pre[...] += dot(x, fake[...])

    @pl.when(i == T - 1)
    def _():
        v = tg[...]
        th[...] = (v * jax.nn.sigmoid(v) * tu[...]).astype(BF16)
        v = gate_pre[...]
        hidden[...] = (v * jax.nn.sigmoid(v) * up_pre[...]).astype(BF16)

    @pl.when(i >= T)
    def _():
        prepare_steps(ds, sd_scr, rd_scr)
        quantize(dw, sd_scr, rd_scr, fake_d)
        partial[...] = (dot(hidden[...], fake_d[...]) - dot(th[...], dw[...])).astype(BF16)


def backward_kernel(
    T, err, tok, hidden, gate_pre, up_pre, gw, uw, dw, gs, us, ds,
    gg, ug, dg, gsg, usg, dsg,
    hidden_t, hg, gpg, upg, s_scr, r_scr, sd_scr, rd_scr, full, full_d, fake_d,
):
    i = pl.program_id(0)

    @pl.when(i == 0)
    def _():
        hidden_t[...] = hidden[...].T
        hg[...] = jnp.zeros_like(hg)

    @pl.when(i < T)
    def _():
        e = err[...]
        full_d[...] = dot(hidden_t[...], e)
        prepare_steps(ds, sd_scr, rd_scr)
        latent(dw, sd_scr, rd_scr, full_d, dg, dsg, fake_d)
        hg[...] += lax.dot_general(
            e, fake_d[...], (((1,), (1,)), ((), ())), preferred_element_type=F32
        )

    @pl.when(i == T)
    def _():
        v = gate_pre[...]
        sigma = jax.nn.sigmoid(v)
        h = hg[...]
        gpg[...] = (h * up_pre[...] * sigma * (1.0 + v * (1.0 - sigma))).astype(BF16)
        upg[...] = (h * (v * sigma)).astype(BF16)

    @pl.when(i >= T)
    def _():
        xt = tok[...].T
        for w, s, pg, grad, step in ((gw, gs, gpg, gg, gsg), (uw, us, upg, ug, usg)):
            full[...] = dot(xt, pg[...])
            prepare_steps(s, s_scr, r_scr)
            latent(w, s_scr, r_scr, full, grad, step)


def specs(T, tile, rows, ff, early):
    a = (lambda i: jnp.minimum(i, T - 1)) if early else (lambda i: jnp.maximum(i - T, 0))
    b = (lambda i: jnp.maximum(i - T, 0)) if early else (lambda i: jnp.minimum(i, T - 1))
    return {
        "tok": pl.BlockSpec((rows, tile), lambda i: (0, a(i))),
        "wide": pl.BlockSpec((tile, ff), lambda i: (a(i), 0)),
        "wide_step": pl.BlockSpec((tile // GROUP, ff), lambda i: (a(i), 0)),
        "down": pl.BlockSpec((ff, tile), lambda i: (0, b(i))),
        "down_step": pl.BlockSpec((ff // GROUP, tile), lambda i: (0, b(i))),
        "rows": pl.BlockSpec((rows, tile), lambda i: (0, b(i))),
        "whole": pl.BlockSpec((rows, ff), lambda i: (0, 0)),
    }


def step_scratch(tile, ff):
    return [
        pltpu.VMEM((tile // GROUP, ff), F32),
        pltpu.VMEM((tile // GROUP, ff), F32),
        pltpu.VMEM((ff // GROUP, tile), F32),
        pltpu.VMEM((ff // GROUP, tile), F32),
    ]


def body(tokens, gate_weight, up_weight, down_weight, gate_step, up_step, down_step, *, count):
    D, ff = gate_weight.shape
    tile = 512
    T = D // tile
    whole = gather_tokens(tokens, count)
    rows = whole.shape[0]
    shape = jax.ShapeDtypeStruct
    params = pltpu.CompilerParams(
        dimension_semantics=("arbitrary",), vmem_limit_bytes=VMEM_LIMIT
    )
    b = specs(T, tile, rows, ff, True)
    partial, gate_pre, up_pre, hidden = pl.pallas_call(
        functools.partial(forward_kernel, T),
        grid=(2 * T,),
        in_specs=[b["tok"], b["wide"], b["wide"], b["down"],
                  b["wide_step"], b["wide_step"], b["down_step"]],
        out_specs=[b["rows"], b["whole"], b["whole"], b["whole"]],
        out_shape=[shape((rows, D), BF16), shape((rows, ff), F32),
                   shape((rows, ff), F32), shape((rows, ff), BF16)],
        scratch_shapes=[
            pltpu.VMEM((rows, ff), F32), pltpu.VMEM((rows, ff), F32), pltpu.VMEM((rows, ff), BF16),
            *step_scratch(tile, ff),
            pltpu.VMEM((tile, ff), BF16), pltpu.VMEM((ff, tile), BF16),
        ],
        compiler_params=params,
        name="forward",
    )(whole, gate_weight, up_weight, down_weight, gate_step, up_step, down_step)
    error = sum_gather(partial, count)
    b = specs(T, tile, rows, ff, False)
    return tuple(pl.pallas_call(
        functools.partial(backward_kernel, T),
        grid=(2 * T,),
        in_specs=[b["rows"], b["tok"], b["whole"], b["whole"], b["whole"],
                  b["wide"], b["wide"], b["down"],
                  b["wide_step"], b["wide_step"], b["down_step"]],
        out_specs=[b["wide"], b["wide"], b["down"],
                   b["wide_step"], b["wide_step"], b["down_step"]],
        out_shape=[shape((D, ff), BF16), shape((D, ff), BF16), shape((ff, D), BF16),
                   shape(gate_step.shape, F32), shape(up_step.shape, F32),
                   shape(down_step.shape, F32)],
        scratch_shapes=[
            pltpu.VMEM((ff, rows), BF16), pltpu.VMEM((rows, ff), F32),
            pltpu.VMEM((rows, ff), BF16), pltpu.VMEM((rows, ff), BF16),
            *step_scratch(tile, ff),
            pltpu.VMEM((tile, ff), F32), pltpu.VMEM((ff, tile), F32), pltpu.VMEM((ff, tile), BF16),
        ],
        compiler_params=params,
        name="backward",
    )(error, whole, hidden, gate_pre, up_pre, gate_weight, up_weight, down_weight,
      gate_step, up_step, down_step))


def solution(mesh):
    return jax.shard_map(
        functools.partial(body, count=mesh.shape["tensor"]),
        mesh=mesh,
        in_specs=(
            P(("groups", "tensor"), None),
            P("groups", "tensor"),
            P("groups", "tensor"),
            P(("groups", "tensor"), None),
            P("groups", "tensor"),
            P("groups", "tensor"),
            P(("groups", "tensor"), None),
        ),
        out_specs=(
            P("groups", "tensor"),
            P("groups", "tensor"),
            P(("groups", "tensor"), None),
            P("groups", "tensor"),
            P("groups", "tensor"),
            P(("groups", "tensor"), None),
        ),
        check_vma=False,
    )
```

time: 362 us -> 105 us (0.29)
  local copies, waits for them, and re-layouts: 149 us -> 0 us
  Pallas kernels: 0 us -> 103 us
  waiting for transfers between devices: 77.6 us -> 0 us
  matrix products: 75.3 us -> 0 us
  other arithmetic: 43.5 us -> 0 us
  between operations: 13.9 us -> 0.65 us
    pallas_call x0 -> x4, Pallas kernels: none -> 103 us  [the longest x1 31.6 us: body(): pl.pallas_call(functools.partial(backward_kernel, T), grid=(2 * T,), in_s...]
    dot_general x9 -> x0, matrix products: 75.3 us -> none  [the longest x1 13.9 us: body(): lax.dot_general(whole, gate_pre_grad, (((0,), (0,)), ((), ())), preferred...]
    reduce_scatter x1 -> x0, waiting for transfers between devices: 64.3 us -> none  [body(): lax.psum_scatter(jnp.dot(hidden_rows, down_fake, preferred_element_type=j...]
    unnamed x44 -> x0, local copies, waits for them, and re-layouts: 48.2 us -> none
    div x4 -> x0, local copies, waits for them, and re-layouts: 44.5 us -> none  [fake_quant(): weight.astype(jnp.float32).reshape(group_count, -1, columns) / step_wide]
    dot_general x2 -> x0, local copies, waits for them, and re-layouts: 32.5 us -> none  [the longest x1 16.3 us: body(): lax.dot_general(whole, gate_pre_grad, (((0,), (0,)), ((), ())), preferred...]
    reduce_sum x3 -> x0, other arithmetic: 30.3 us -> none  [latent_grads(): jnp.sum(shaped * step_slope, axis=1)]
    convert_element_type x2 -> x0, local copies, waits for them, and re-layouts: 23.6 us -> none  [fake_quant(): weight.astype(jnp.float32).reshape(group_count, -1, columns) / step_wide]
  transfers between devices with their start and end apart: 3 -> 0, of which waited for: 2 -> 0; matrix products, arithmetic and copies ran while one was open for 28% -> 0% of each run, Pallas kernels for 0% -> 0%
where the time goes in v1:
time: 105 us; the launch traced here: 104 us
  Pallas kernels  103 us (98%)
    pallas_call x1, Pallas kernels, body(): pl.pallas_call(functools.partial(backward_kernel, T), grid=(2 * T,), in_s...  31.6 us
    pallas_call x1, Pallas kernels, sum_gather(): pl.pallas_call(functools.partial(sum_gather_kernel, Z, Y), out_shape=jax....  27.9 us
    pallas_call x1, Pallas kernels, body(): pl.pallas_call(functools.partial(forward_kernel, T), grid=(2 * T,), in_sp...  24.9 us
    pallas_call x1, Pallas kernels, gather_tokens(): pl.pallas_call(functools.partial(gather_kernel, Z, Y), out_shape=jax.Shap...  19 us

profile of v1, /device:TPU:0, one launch (start us, length us, event | category | flops | bytes accessed | tf_op | source)
XLA Modules:
  0.0 104.1 jit_solution(15684702011971818856)
XLA Ops:
  0.6 19.0 %gather_tokens.1 = bf16[4,2,2,8,4096]{4,3,2,1,0:T(8,128)(2,1)} custom-call(bf16[8,4096]{1,0:T(8,128)(2,1)} %x_ref.1), custom_call_target="tpu_custom_call" | custom-call | tf_op jit(solution)/shard_map/gather_tokens/pallas_call | solution.py:155
  19.6 24.9 %forward.1 = (bf16[128,4096]{1,0:T(8,128)(2,1)}, f32[128,896]{1,0:T(8,128)}, f32[128,896]{1,0:T(8,128)}, bf16[128,896]{1,0:T(8,128)(2,1)}) custom-call(bf16[128,4096]{1,0:T(8,128)(2,1)} %bitcast.3, bf16[4096,896]{1,0:T(8,128)(2,1)} %gw.3, bf16[4096,896]{1,0:T(8,128)(2,1)} %uw.3, bf16[896,4096]{1,0:T(8,128)(2,1)} %dw.3, bf16[128,896]{1,0:T(8,128)(2,1)} %gs.3, ...), custom_call_target="tpu_custom_call" | custom-call | tf_op jit(solution)/shard_map/forward/pallas_call | solution.py:341
  44.5 27.9 %sum_gather_error.1 = bf16[4,2,2,8,4096]{4,3,2,1,0:T(8,128)(2,1)} custom-call(bf16[4,2,2,8,4096]{4,3,2,1,0:T(8,128)(2,1)} %bitcast.6), custom_call_target="tpu_custom_call" | custom-call | tf_op jit(solution)/shard_map/sum_gather_error/pallas_call | solution.py:176
  72.4 31.6 %backward.1 = (bf16[4096,896]{1,0:T(8,128)(2,1)}, bf16[4096,896]{1,0:T(8,128)(2,1)}, bf16[896,4096]{1,0:T(8,128)(2,1)}, f32[128,896]{1,0:T(8,128)}, f32[128,896]{1,0:T(8,128)}, /*index=5*/f32[28,4096]{1,0:T(8,128)}) custom-call(bf16[128,4096]{1,0:T(8,128)(2,1)} %bitcast.5, bf16[128,4096]{1,0:T(8,128)(2,1)} %bitcast.4, ...), custom_call_target="tpu_custom_call" | custom-call | tf_op jit(solution)/shard_map/backward/pallas_call | solution.py:359

commit v2 on v1

v2 whole, which is shorter than its diff:
```python
import functools
import math

import jax
import jax.numpy as jnp
from jax import lax
from jax.experimental import pallas as pl
from jax.experimental.pallas import tpu as pltpu
from jax.sharding import PartitionSpec as P

F32 = jnp.float32
BF16 = jnp.bfloat16
MESH = pl.DeviceIdType.MESH
GROUP = 32
CHUNKS = 4
VMEM_LIMIT = 56 * 1024 * 1024


def place(Z, Y):
    me = lax.axis_index("tensor")
    core = lax.rem(me, 2)
    y = lax.rem(me // 2, Y)
    z = me // (2 * Y)
    return z, y, core


def meet(Z, Y, z, y, core):
    peers = [(lax.rem(z + d, Z) * Y + y) * 2 + core for d in range(1, Z)]
    peers.append((z * Y + (1 - y)) * 2 + core)
    peers.append((z * Y + y) * 2 + (1 - core))
    barrier = pltpu.get_barrier_semaphore()
    for peer in peers:
        pl.semaphore_signal(barrier, inc=1, device_id={"tensor": peer}, device_id_type=MESH)
    pl.semaphore_wait(barrier, len(peers))
    return peers


def remote(src, dst, send, recv, peer):
    return pltpu.make_async_remote_copy(
        src_ref=src, dst_ref=dst, send_sem=send, recv_sem=recv,
        device_id={"tensor": peer}, device_id_type=MESH,
    )


def spread_line(out, cols, sems, k, base, Z, z, y, core, peers):
    send, recv = sems
    copies = []
    for d in range(Z - 1):
        part = out.at[z, y, core, :, cols]
        copies.append(remote(part, part, send.at[k, base + d], recv.at[k, base + d], peers[d]))
        copies[-1].start()
    return copies


def spread_rest(out, chunks, line, sems, base, Z, z, y, core, peers, work):
    send, recv = sems
    rows, pair = [], []
    for k, cols in enumerate(chunks):
        work()
        for copy in line[k]:
            copy.wait_recv()
        part = out.at[:, y, core, :, cols]
        rows.append(remote(part, part, send.at[k, base], recv.at[k, base], peers[Z - 1]))
        rows[-1].start()
    for k, cols in enumerate(chunks):
        work()
        rows[k].wait_recv()
        part = out.at[:, :, core, :, cols]
        pair.append(remote(part, part, send.at[k, base + 1], recv.at[k, base + 1], peers[Z]))
        pair[-1].start()
    for k in range(len(chunks)):
        work()
        pair[k].wait_recv()
    return rows + pair


def split_axis(count):
    return count // 4, 2


def quantize(w_ref, s_scr, base, groups, fake):
    @pl.loop(0, groups)
    def _(g):
        rows = pl.ds(pl.multiple_of(g * GROUP, GROUP), GROUP)
        step = s_scr[pl.ds(base + g, 1), :]
        scaled = w_ref[rows, :].astype(F32) * (1.0 / step)
        levels = jnp.floor(jnp.clip(scaled, -8.0, 7.0) + 0.5)
        fake[rows, :] = (levels * step).astype(BF16)


def slope_in_place(w_ref, s_scr, base, groups):
    @pl.loop(0, groups)
    def _(g):
        rows = pl.ds(pl.multiple_of(g * GROUP, GROUP), GROUP)
        scaled = w_ref[rows, :].astype(F32) * (1.0 / s_scr[pl.ds(base + g, 1), :])
        clipped = jnp.clip(scaled, -8.0, 7.0)
        levels = jnp.floor(clipped + 0.5)
        slope = levels - jnp.where(clipped == scaled, scaled, 0.0)
        w_ref[rows, :] = slope.astype(BF16)


def latent(slope_ref, full, grad_ref, step_ref):
    factor = 1.0 / math.sqrt(GROUP * 7.0)
    for g in range(step_ref.shape[0]):
        rows = pl.ds(g * GROUP, GROUP)
        slope = slope_ref[rows, :].astype(F32)
        part = full[rows, :]
        grad_ref[rows, :] = jnp.where(jnp.abs(slope) <= 0.5, part, 0.0).astype(BF16)
        step_ref[pl.ds(g, 1), :] = jnp.sum(part * slope, axis=0, keepdims=True) * factor


def dot(a, b):
    return jnp.dot(a, b, preferred_element_type=F32)


def front_kernel(
    Z, Y, T, x_ref, gw, uw, dw, gs, us, ds,
    out_x, out, gate_pre, up_pre, hidden, slope_g, slope_u, slope_d, out_fd,
    w_g, w_u, w_d, f_g, f_u, f_d, s_g, s_u, s_d, x2d, tg, tu, th,
    p_ref, from_core, to_y, mine, from_y, to_z, from_z,
    in_sem, out_sem, send0, recv0, send, recv,
):
    z, y, core = place(Z, Y)
    D, ff = gw.shape
    rows = x2d.shape[1]
    tile = D // T
    wide = [pl.ds(t * tile, tile) for t in range(T)]
    width = D // CHUNKS
    chunks = [pl.ds(k * width, width) for k in range(CHUNKS)]

    loads = {}
    for t in range(T):
        loads["d", t] = pltpu.make_async_copy(dw.at[:, wide[t]], w_d.at[t], in_sem.at[2, t])
        loads["g", t] = pltpu.make_async_copy(gw.at[wide[t], :], w_g.at[t], in_sem.at[0, t])
        loads["u", t] = pltpu.make_async_copy(uw.at[wide[t], :], w_u.at[t], in_sem.at[1, t])
    order = [("d", t) for t in range(T)] + [(n, t) for t in range(T) for n in "gu"]
    for key in order:
        loads[key].start()
    out_x[z, y, core] = x_ref[...]
    peers = meet(Z, Y, z, y, core)
    line = [
        spread_line(out_x, cols, (send0, recv0), k, 0, Z, z, y, core, peers)
        for k, cols in enumerate(chunks)
    ]
    s_g[...] = gs[...].astype(F32)
    s_u[...] = us[...].astype(F32)
    for t in range(T):
        s_d[t] = ds[:, wide[t]].astype(F32)

    weights = {"g": (w_g, f_g, s_g, slope_g), "u": (w_u, f_u, s_u, slope_u),
               "d": (w_d, f_d, s_d, slope_d)}
    stores = []

    def pick(name, t):
        w, f, s, target = weights[name]
        if name == "d":
            return w.at[t], f.at[t], s.at[t], 0, ff // GROUP, target.at[:, wide[t]]
        return w.at[t], f.at[t], s, t * (tile // GROUP), tile // GROUP, target.at[wide[t], :]

    def quantize_one(key):
        loads[key].wait()
        w, f, s, base, groups, _ = pick(*key)
        quantize(w, s, base, groups, f)
        if key[0] == "d":
            copy = pltpu.make_async_copy(f, out_fd.at[:, wide[key[1]]], out_sem.at[3, key[1]])
            copy.start()
            stores.append(copy)

    def slope_one(key):
        w, _, s, base, groups, target = pick(*key)
        slope_in_place(w, s, base, groups)
        copy = pltpu.make_async_copy(w, target, out_sem.at["gud".index(key[0]), key[1]])
        copy.start()
        stores.append(copy)

    def worker(do, each):
        left = list(order)

        def work(count=each):
            for key in left[:count]:
                do(key)
            del left[:count]

        return work

    work = worker(quantize_one, 2)
    ends = [spread_rest(out_x, chunks, line, (send0, recv0), Z - 1, Z, z, y, core, peers, work)]
    ends += line
    work(3 * T)

    for t in range(T):
        x2d[t] = out_x[:, :, :, :, wide[t]].astype(F32).reshape(rows, tile).astype(BF16)
    for ref in (tg, tu, gate_pre, up_pre):
        ref[...] = jnp.zeros_like(ref)

    @pl.loop(0, T)
    def _(t):
        x = x2d[t]
        tg[...] += dot(x, w_g[t])
        tu[...] += dot(x, w_u[t])
        gate_pre[...] += dot(x, f_g[t])
        up_pre[...] += dot(x, f_u[t])

    v = tg[...]
    th[...] = (v * jax.nn.sigmoid(v) * tu[...]).astype(BF16)
    v = gate_pre[...]
    hidden[...] = (v * jax.nn.sigmoid(v) * up_pre[...]).astype(BF16)

    first = []
    per = T // CHUNKS
    for k, cols in enumerate(chunks):
        for t in range(k * per, (k + 1) * per):
            part = dot(hidden[...], f_d[t]) - dot(th[...], w_d[t])
            p_ref[:, :, :, :, wide[t]] = part.reshape(Z, Y, 2, rows // (4 * Z), tile).astype(BF16)
        copy = remote(
            p_ref.at[:, :, 1 - core, :, cols], from_core.at[:, :, :, cols],
            send.at[k, 0], recv.at[k, 0], peers[Z],
        )
        copy.start()
        first.append(copy)

    work = worker(slope_one, 1)
    second = []
    for k, cols in enumerate(chunks):
        first[k].wait_recv()
        for i in range(Z):
            to_y[i, :, cols] = (
                p_ref[i, 1 - y, core, :, cols].astype(F32)
                + from_core[i, 1 - y, :, cols].astype(F32)
            ).astype(BF16)
        copy = remote(
            to_y.at[:, :, cols], from_y.at[:, :, cols], send.at[k, 1], recv.at[k, 1], peers[Z - 1]
        )
        copy.start()
        second.append(copy)
        for i in range(Z):
            mine[i, :, cols] = (
                p_ref[i, y, core, :, cols].astype(F32) + from_core[i, y, :, cols].astype(F32)
            )
    third = []
    for k, cols in enumerate(chunks):
        work()
        second[k].wait_recv()
        for i in range(Z):
            mine[i, :, cols] = mine[i, :, cols] + from_y[i, :, cols].astype(F32)
        third.append([])
        for d in range(Z - 1):
            there = lax.rem(z + d + 1, Z)
            to_z[d, :, cols] = mine[there, :, cols].astype(BF16)
            copy = remote(
                to_z.at[d, :, cols], from_z.at[d, :, cols],
                send.at[k, 2 + d], recv.at[k, 2 + d], peers[d],
            )
            copy.start()
            third[k].append(copy)
    line = []
    for k, cols in enumerate(chunks):
        work()
        total = mine[z, :, cols]
        for d in range(Z - 1):
            third[k][d].wait_recv()
            total = total + from_z[d, :, cols].astype(F32)
        out[z, y, core, :, cols] = total.astype(BF16)
        line.append(spread_line(out, cols, (send, recv), k, Z + 1, Z, z, y, core, peers))
    ends.append(spread_rest(out, chunks, line, (send, recv), 2 * Z, Z, z, y, core, peers, work))
    work(3 * T)
    ends += line + third + [first, second, stores]
    for group in ends:
        for copy in group:
            if group is stores:
                copy.wait()
            else:
                copy.wait_send()


def backward_kernel(
    T, err, tok, hidden, gate_pre, up_pre, gl, ul, dl, fd,
    gg, ug, dg, gsg, usg, dsg,
    hidden_t, hg, gpg, upg, full, full_d,
):
    i = pl.program_id(0)

    @pl.when(i == 0)
    def _():
        hidden_t[...] = hidden[...].T
        hg[...] = jnp.zeros_like(hg)

    @pl.when(i < T)
    def _():
        e = err[...]
        full_d[...] = dot(hidden_t[...], e)
        hg[...] += lax.dot_general(
            e, fd[...], (((1,), (1,)), ((), ())), preferred_element_type=F32
        )
        latent(dl, full_d, dg, dsg)

    @pl.when(i == T)
    def _():
        v = gate_pre[...]
        sigma = jax.nn.sigmoid(v)
        h = hg[...]
        gpg[...] = (h * up_pre[...] * sigma * (1.0 + v * (1.0 - sigma))).astype(BF16)
        upg[...] = (h * (v * sigma)).astype(BF16)

    @pl.when(i >= T)
    def _():
        xt = tok[...].T
        for sl, pg, grad, step in ((gl, gpg, gg, gsg), (ul, upg, ug, usg)):
            full[...] = dot(xt, pg[...])
            latent(sl, full, grad, step)


def specs(T, tile, rows, ff, early):
    a = (lambda i: jnp.minimum(i, T - 1)) if early else (lambda i: jnp.maximum(i - T, 0))
    b = (lambda i: jnp.maximum(i - T, 0)) if early else (lambda i: jnp.minimum(i, T - 1))
    return {
        "tok": pl.BlockSpec((rows, tile), lambda i: (0, a(i))),
        "wide": pl.BlockSpec((tile, ff), lambda i: (a(i), 0)),
        "wide_step": pl.BlockSpec((tile // GROUP, ff), lambda i: (a(i), 0)),
        "down": pl.BlockSpec((ff, tile), lambda i: (0, b(i))),
        "down_step": pl.BlockSpec((ff // GROUP, tile), lambda i: (0, b(i))),
        "rows": pl.BlockSpec((rows, tile), lambda i: (0, b(i))),
        "whole": pl.BlockSpec((rows, ff), lambda i: (0, 0)),
    }


def body(tokens, gate_weight, up_weight, down_weight, gate_step, up_step, down_step, *, count):
    D, ff = gate_weight.shape
    tile = 512
    T = D // tile
    Z, Y = split_axis(count)
    part = tokens.shape[0]
    rows = part * count
    shape = jax.ShapeDtypeStruct
    vmem = pl.BlockSpec(memory_space=pltpu.VMEM)
    hbm = pl.BlockSpec(memory_space=pl.ANY)
    whole, error, gate_pre, up_pre, hidden, slope_g, slope_u, slope_d, fake_d = pl.pallas_call(
        functools.partial(front_kernel, Z, Y, T),
        in_specs=[vmem, hbm, hbm, hbm, vmem, vmem, vmem],
        out_specs=[vmem] * 5 + [hbm] * 4,
        out_shape=[
            shape((Z, Y, 2, part, D), BF16), shape((Z, Y, 2, part, D), BF16),
            shape((rows, ff), F32), shape((rows, ff), F32), shape((rows, ff), BF16),
            shape((D, ff), BF16), shape((D, ff), BF16), shape((ff, D), BF16), shape((ff, D), BF16),
        ],
        scratch_shapes=[
            pltpu.VMEM((T, tile, ff), BF16), pltpu.VMEM((T, tile, ff), BF16),
            pltpu.VMEM((T, ff, tile), BF16),
            pltpu.VMEM((T, tile, ff), BF16), pltpu.VMEM((T, tile, ff), BF16),
            pltpu.VMEM((T, ff, tile), BF16),
            pltpu.VMEM((D // GROUP, ff), F32), pltpu.VMEM((D // GROUP, ff), F32),
            pltpu.VMEM((T, ff // GROUP, tile), F32),
            pltpu.VMEM((T, rows, tile), BF16),
            pltpu.VMEM((rows, ff), F32), pltpu.VMEM((rows, ff), F32), pltpu.VMEM((rows, ff), BF16),
            pltpu.VMEM((Z, Y, 2, part, D), BF16),
            pltpu.VMEM((Z, Y, part, D), BF16),
            pltpu.VMEM((Z, part, D), BF16),
            pltpu.VMEM((Z, part, D), F32),
            pltpu.VMEM((Z, part, D), BF16),
            pltpu.VMEM((Z - 1, part, D), BF16),
            pltpu.VMEM((Z - 1, part, D), BF16),
            pltpu.SemaphoreType.DMA((3, T)),
            pltpu.SemaphoreType.DMA((4, T)),
            pltpu.SemaphoreType.DMA((CHUNKS, Z + 1)),
            pltpu.SemaphoreType.DMA((CHUNKS, Z + 1)),
            pltpu.SemaphoreType.DMA((CHUNKS, 2 * Z + 2)),
            pltpu.SemaphoreType.DMA((CHUNKS, 2 * Z + 2)),
        ],
        compiler_params=pltpu.CompilerParams(
            collective_id=0, has_side_effects=True, vmem_limit_bytes=60 * 1024 * 1024
        ),
        name="front",
    )(tokens, gate_weight, up_weight, down_weight, gate_step, up_step, down_step)
    whole = whole.reshape(rows, D)
    error = error.reshape(rows, D)
    b = specs(T, tile, rows, ff, False)
    return tuple(pl.pallas_call(
        functools.partial(backward_kernel, T),
        grid=(2 * T,),
        in_specs=[b["rows"], b["tok"], b["whole"], b["whole"], b["whole"],
                  b["wide"], b["wide"], b["down"], b["down"]],
        out_specs=[b["wide"], b["wide"], b["down"],
                   b["wide_step"], b["wide_step"], b["down_step"]],
        out_shape=[shape((D, ff), BF16), shape((D, ff), BF16), shape((ff, D), BF16),
                   shape(gate_step.shape, F32), shape(up_step.shape, F32),
                   shape(down_step.shape, F32)],
        scratch_shapes=[
            pltpu.VMEM((ff, rows), BF16), pltpu.VMEM((rows, ff), F32),
            pltpu.VMEM((rows, ff), BF16), pltpu.VMEM((rows, ff), BF16),
            pltpu.VMEM((tile, ff), F32), pltpu.VMEM((ff, tile), F32),
        ],
        compiler_params=pltpu.CompilerParams(
            dimension_semantics=("arbitrary",), vmem_limit_bytes=VMEM_LIMIT
        ),
        name="backward",
    )(error, whole, hidden, gate_pre, up_pre, slope_g, slope_u, slope_d, fake_d))


def solution(mesh):
    return jax.shard_map(
        functools.partial(body, count=mesh.shape["tensor"]),
        mesh=mesh,
        in_specs=(
            P(("groups", "tensor"), None),
            P("groups", "tensor"),
            P("groups", "tensor"),
            P(("groups", "tensor"), None),
            P("groups", "tensor"),
            P("groups", "tensor"),
            P(("groups", "tensor"), None),
        ),
        out_specs=(
            P("groups", "tensor"),
            P("groups", "tensor"),
            P(("groups", "tensor"), None),
            P("groups", "tensor"),
            P("groups", "tensor"),
            P(("groups", "tensor"), None),
        ),
        check_vma=False,
    )
```

time: 105 us -> 92.3 us (0.88)
  Pallas kernels: 103 us -> 91.1 us
    pallas_call x3 -> x1, Pallas kernels: 71.8 us -> 63.1 us  [body(): pl.pallas_call(functools.partial(front_kernel, Z, Y, T), in_specs=[vmem,...]
    pallas_call x1, Pallas kernels: 31.6 us -> 28 us  [body(): pl.pallas_call(functools.partial(backward_kernel, T), grid=(2 * T,), in_s...]
where the time goes in v2:
time: 92.3 us; the launch traced here: 91.8 us
  Pallas kernels  91.1 us (99%)
    pallas_call x1, Pallas kernels, body(): pl.pallas_call(functools.partial(front_kernel, Z, Y, T), in_specs=[vmem,...  63.1 us
    pallas_call x1, Pallas kernels, body(): pl.pallas_call(functools.partial(backward_kernel, T), grid=(2 * T,), in_s...  28 us

profile of v2, /device:TPU:0, one launch (start us, length us, event | category | flops | bytes accessed | tf_op | source)
XLA Modules:
  0.0 91.8 jit_solution(12714071698027690436)
XLA Ops:
  0.6 63.1 %front.1 = (bf16[4,2,2,8,4096]{4,3,2,1,0:T(8,128)(2,1)}, bf16[4,2,2,8,4096]{4,3,2,1,0:T(8,128)(2,1)}, f32[128,896]{1,0:T(8,128)}, f32[128,896]{1,0:T(8,128)}, bf...) custom-call(bf16[8,4096]{1,0:T(8,128)(2,1)} %x_ref.1, ...), custom_call_target="tpu_custom_call" | custom-call | tf_op jit(solution)/shard_map/front/pallas_call | solution.py:337
  63.7 28.0 %backward.1 = (bf16[4096,896]{1,0:T(8,128)(2,1)}, bf16[4096,896]{1,0:T(8,128)(2,1)}, bf16[896,4096]{1,0:T(8,128)(2,1)}, f32[128,896]{1,0:T(8,128)}, f32[128,896]{1,0:T(8,128)}, /*index=5*/f32[28,4096]{1,0:T(8,128)}) custom-call(bf16[128,4096]{1,0:T(8,128)(2,1)} %bitcast.3, bf16[128,4096]{1,0:T(8,128)(2,1)} %bitcast.2, ...), custom_call_target="tpu_custom_call" | custom-call | tf_op jit(solution)/shard_map/backward/pallas_call | solution.py:377

commit v3 on v2

--- a/solution.py
+++ b/solution.py
@@ -79,7 +79,7 @@
 
 
 def quantize(w_ref, s_scr, base, groups, fake):
-    @pl.loop(0, groups)
+    @pl.loop(0, groups, unroll=4)
     def _(g):
         rows = pl.ds(pl.multiple_of(g * GROUP, GROUP), GROUP)
         step = s_scr[pl.ds(base + g, 1), :]
@@ -89,7 +89,7 @@
 
 
 def slope_in_place(w_ref, s_scr, base, groups):
-    @pl.loop(0, groups)
+    @pl.loop(0, groups, unroll=4)
     def _(g):
         rows = pl.ds(pl.multiple_of(g * GROUP, GROUP), GROUP)
         scaled = w_ref[rows, :].astype(F32) * (1.0 / s_scr[pl.ds(base + g, 1), :])
@@ -373,6 +373,8 @@
     )(tokens, gate_weight, up_weight, down_weight, gate_step, up_step, down_step)
     whole = whole.reshape(rows, D)
     error = error.reshape(rows, D)
+    tile = 1024
+    T = D // tile
     b = specs(T, tile, rows, ff, False)
     return tuple(pl.pallas_call(
         functools.partial(backward_kernel, T),

time: 92.3 us -> 88.9 us (0.963)
  Pallas kernels: 91.1 us -> 88 us
    pallas_call x1, Pallas kernels: 28 us -> 26 us  [body(): pl.pallas_call(functools.partial(backward_kernel, T), grid=(2 * T,), in_s...]
    pallas_call x1, Pallas kernels: 63.1 us -> 62 us  [body(): pl.pallas_call(functools.partial(front_kernel, Z, Y, T), in_specs=[vmem,...]
where the time goes in v3:
time: 88.9 us; the launch traced here: 88.8 us
  Pallas kernels  88 us (99%)
    pallas_call x1, Pallas kernels, body(): pl.pallas_call(functools.partial(front_kernel, Z, Y, T), in_specs=[vmem,...  62 us
    pallas_call x1, Pallas kernels, body(): pl.pallas_call(functools.partial(backward_kernel, T), grid=(2 * T,), in_s...  26 us

profile of v3, /device:TPU:0, one launch (start us, length us, event | category | flops | bytes accessed | tf_op | source)
XLA Modules:
  0.0 88.8 jit_solution(1906017221857613903)
XLA Ops:
  0.6 62.0 %front.1 = (bf16[4,2,2,8,4096]{4,3,2,1,0:T(8,128)(2,1)}, bf16[4,2,2,8,4096]{4,3,2,1,0:T(8,128)(2,1)}, f32[128,896]{1,0:T(8,128)}, f32[128,896]{1,0:T(8,128)}, bf...) custom-call(bf16[8,4096]{1,0:T(8,128)(2,1)} %x_ref.1, ...), custom_call_target="tpu_custom_call" | custom-call | tf_op jit(solution)/shard_map/front/pallas_call | solution.py:337
  62.6 26.0 %backward.1 = (bf16[4096,896]{1,0:T(8,128)(2,1)}, bf16[4096,896]{1,0:T(8,128)(2,1)}, bf16[896,4096]{1,0:T(8,128)(2,1)}, f32[128,896]{1,0:T(8,128)}, f32[128,896]{1,0:T(8,128)}, /*index=5*/f32[28,4096]{1,0:T(8,128)}) custom-call(bf16[128,4096]{1,0:T(8,128)(2,1)} %bitcast.3, bf16[128,4096]{1,0:T(8,128)(2,1)} %bitcast.2, ...), custom_call_target="tpu_custom_call" | custom-call | tf_op jit(solution)/shard_map/backward/pallas_call | solution.py:379
